TPU v7x, 256 devices: a whole 4x4x8 slice. The times are simulated.
256 devices in a mesh: mp: 32 (over z, x), dp: 8 (over y, core).
Axes of the slice: x: 4, y: 4, z: 8, core: 2. Of those that a mesh axis runs over, the one named last changes fastest.
Arguments:
- inputs: bfloat16 [1536, 8192], P('dp', 'mp'), may hold values from -42 to 42
- out_grads: bfloat16 [1536, 16384], P('dp', 'mp'), may hold values from -42 to 42
- weight: bfloat16 [8192, 16384], P('dp', 'mp'), may hold values from -0.25 to 0.25
- enc_in: bfloat16 [8192, 1920], P('mp'), may hold values from -0.0625 to 0.0625
- dec_in: bfloat16 [1920, 8192], P(None, 'mp'), may hold values from -0.125 to 0.125
- enc_out: bfloat16 [16384, 1920], P('mp'), may hold values from -0.046875 to 0.046875
- dec_out: bfloat16 [1920, 16384], P(None, 'mp'), may hold values from -0.125 to 0.125
Outputs:
- post_out: bfloat16 [1536, 16384], P('dp', 'mp')
- grad_in: bfloat16 [1536, 8192], P('dp', 'mp')
All inputs are finite; a program needn't handle non-finite values.
Results may differ from a plain program's by a relative error of at most 0.024.
Values may be sent and summed in bfloat16 or wider, within the bound.
A program may use at most 64 MiB of HBM per device.

v0:
```python
import jax
import jax.numpy as jnp
from jax import lax
from jax.sharding import PartitionSpec as P

D = 8192
FW = 16384
epsilon = 1e-06
step_size = 0.25


def silu_slope(value):
    sig = jax.nn.sigmoid(value)
    return sig * (1.0 + value * (1.0 - sig))


def shards(inputs, out_grads, weight, enc_in, dec_in, enc_out, dec_out):
    factor = step_size / D
    input_wide = inputs.astype(jnp.float32)
    grad_wide = out_grads.astype(jnp.float32)
    input_sq = jnp.sum(input_wide * input_wide, axis=1)
    grad_sq = jnp.sum(grad_wide * grad_wide, axis=1)
    input_proj = jnp.dot(inputs, enc_in, preferred_element_type=jnp.float32)
    grad_proj = jnp.dot(out_grads, enc_out, preferred_element_type=jnp.float32)
    input_total, grad_total = lax.psum((input_sq, grad_sq), "mp")
    input_proj, grad_proj = (
        lax.psum(input_proj.astype(jnp.bfloat16), "mp").astype(jnp.float32),
        lax.psum(grad_proj.astype(jnp.bfloat16), "mp").astype(jnp.float32),
    )
    input_scale = lax.rsqrt(input_total / D + epsilon)[:, None]
    grad_scale = lax.rsqrt(grad_total / FW + epsilon)[:, None]
    input_hidden = jax.nn.relu(input_proj * input_scale).astype(jnp.bfloat16)
    grad_hidden = jax.nn.relu(grad_proj * grad_scale).astype(jnp.bfloat16)
    edited_in = (
        input_wide + jnp.dot(input_hidden, dec_in, preferred_element_type=jnp.float32)
    ).astype(jnp.bfloat16)
    edited_grad = (
        grad_wide + jnp.dot(grad_hidden, dec_out, preferred_element_type=jnp.float32)
    ).astype(jnp.bfloat16)
    whole_in = lax.all_gather(inputs, "mp", axis=1, tiled=True)
    edits_all = lax.all_gather(edited_in, "dp", axis=0, tiled=True)
    grads_all = lax.all_gather(edited_grad, "dp", axis=0, tiled=True)
    kernel = lax.psum(
        jnp.dot(inputs, edits_all.T, preferred_element_type=jnp.float32).astype(jnp.bfloat16), "mp"
    ).astype(jnp.float32)
    kernel = (kernel * factor).astype(jnp.bfloat16)
    base_out = jnp.dot(
        whole_in,
        lax.all_gather(weight, "dp", axis=0, tiled=True),
        preferred_element_type=jnp.float32,
    )
    post_full = base_out - jnp.dot(kernel, grads_all, preferred_element_type=jnp.float32)
    cotangent = (grad_wide * silu_slope(post_full)).astype(jnp.bfloat16)
    back_kernel = lax.psum(
        jnp.dot(cotangent, grads_all.T, preferred_element_type=jnp.float32).astype(jnp.bfloat16),
        "mp",
    ).astype(jnp.float32)
    back_kernel = (back_kernel * factor).astype(jnp.bfloat16)
    partial_value = jnp.dot(
        cotangent,
        lax.all_gather(weight, "dp", axis=0, tiled=True).T,
        preferred_element_type=jnp.float32,
    )
    back_sum = lax.psum_scatter(
        partial_value.astype(jnp.bfloat16), "mp", scatter_dimension=1, tiled=True
    ).astype(jnp.float32)
    grad_in = (
        back_sum - jnp.dot(back_kernel, edits_all, preferred_element_type=jnp.float32)
    ).astype(jnp.bfloat16)
    return (post_full.astype(jnp.bfloat16), grad_in)


def solution(mesh):
    in_specs = (
        P("dp", "mp"),
        P("dp", "mp"),
        P("dp", "mp"),
        P("mp", None),
        P(None, "mp"),
        P("mp", None),
        P(None, "mp"),
    )
    out_specs = (P("dp", "mp"), P("dp", "mp"))
    return jax.shard_map(shards, mesh=mesh, in_specs=in_specs, out_specs=out_specs, check_vma=False)
```

profile of v0, /device:TPU:8, one launch (start us, length us, event | category | flops | bytes accessed | tf_op | source)
XLA Modules:
  0.0 874.0 jit_solution(16068317335428372301)
XLA Ops:
  7.2 2.7 convolution_convert_fusion.4
  10.0 0.1 fusion.12
  10.1 0.1 fusion.10
  10.2 77.8 %all-reduce = (f32[192]{0:T(256)S(1)}, f32[192]{0:T(256)S(1)}) all-reduce(f32[192]{0:T(256)S(1)} %fusion.10, f32[192]{0:T(256)S(1)} %fusion.12), channel_id=1, replica_groups=mesh['mp'=32,'dp'=8] {'mp'}, use_global_device_ids=true, to_apply=%region_6.7 | all-reduce | flops 384 | bytes 3072 | tf_op jit(solution)/shard_map/psum | solution.py:25
  88.0 1.5 convolution_convert_fusion.3
  89.5 73.4 %all-reduce.6.cloned.1.call-done = bf16[192,1920]{1,0:T(8,128)(2,1)} async-done(((bf16[192,1920]{1,0:T(8,128)(2,1)}), bf16[192,1920]{1,0:T(8,128)(2,1)}) %all-reduce.6.cloned.1.call-update) | async-done | bytes 737296 | tf_op jit(solution)/shard_map/psum | solution.py:27
  162.9 1.9 fusion.2
  164.8 13.5 %all_gather.15 = bf16[1536,256]{1,0:T(8,128)(2,1)S(1)} all-gather(bf16[192,256]{1,0:T(8,128)(2,1)S(1)} %fusion.2), channel_id=1, replica_groups=mesh['mp'=32,'dp'=8] {'dp'}, dimensions={0}, use_global_device_ids=true | all-gather | bytes 884736 | tf_op jit(solution)/shard_map/all_gather | solution.py:41
  178.3 1.3 fusion
  179.7 0.7 all-gather.4.cloned.1.call-update
  180.4 0.5 all-gather.6.cloned.1.call-update
  181.0 147.2 %all-reduce.10.cloned.1.call-done = (bf16[192,1920]{1,0:T(8,128)(2,1)}, bf16[192,1536]{0,1:T(8,128)(2,1)}) async-done(((bf16[192,1920]{1,0:T(8,128)(2,1)}, bf16[192,1536]{0,1:T(8,128)(2,1)}), (bf16[192,1920]{1,0:T(8,128)(2,1)}, bf16[192,1536]{0,1:T(8,128)(2,1)})) %all-reduce.10.cloned.1.call-update) | async-done | bytes 1327120 | tf_op jit(solution)/shard_map/psum | solution.py:28
  328.2 3.1 fusion.1
  331.3 0.0 all-reduce.8.cloned.1.call-start
  331.4 75.0 %all-gather.4.cloned.1.call-done = bf16[192,8192]{1,0:T(8,128)(2,1)} async-done(((bf16[192,256]{1,0:T(8,128)(2,1)}), bf16[192,8192]{1,0:T(8,128)(2,1)}) %all-gather.4.cloned.1.call-update) | async-done | bytes 3145744 | tf_op jit(solution)/shard_map/all_gather | solution.py:40
  406.4 53.9 %all-gather.6.cloned.1.call-done = bf16[8192,512]{1,0:T(8,128)(2,1)} async-done(((bf16[1024,512]{1,0:T(8,128)(2,1)}), bf16[8192,512]{1,0:T(8,128)(2,1)}) %all-gather.6.cloned.1.call-update) | async-done | bytes 8388624 | tf_op jit(solution)/shard_map/all_gather | solution.py:49
  460.3 6.9 fusion.20
  467.2 22.0 %all-gather.8.cloned.1.call-done = bf16[1536,512]{1,0:T(8,128)(2,1)} async-done(((bf16[192,512]{1,0:T(8,128)(2,1)}), bf16[1536,512]{1,0:T(8,128)(2,1)}) %all-gather.8.cloned.1.call-update) | async-done | bytes 1572880 | tf_op jit(solution)/shard_map/all_gather | solution.py:42
  489.2 2.9 fusion.19
  492.1 2.6 convolution_convert_fusion.2
  494.9 8.1 convolution_convert_fusion
  503.0 142.1 %all-reduce.8.cloned.1.call-done = bf16[192,1536]{0,1:T(8,128)(2,1)} async-done(((bf16[192,1536]{0,1:T(8,128)(2,1)}), bf16[192,1536]{0,1:T(8,128)(2,1)}) %all-reduce.8.cloned.1.call-update) | async-done | bytes 589840 | tf_op jit(solution)/shard_map/psum | solution.py:54
  645.1 219.9 %reduce-scatter.2.cloned.1.call-done = bf16[192,256]{1,0:T(8,128)(2,1)} async-done(((bf16[192,8192]{1,0:T(8,128)(2,1)}), bf16[192,256]{1,0:T(8,128)(2,1)}) %reduce-scatter.2.cloned.1.call-update) | async-done | bytes 98320 | tf_op jit(solution)/shard_map/reduce_scatter | solution.py:64
  865.0 2.2 fusion.3
  (27 shorter events, 0.4 us)
Async XLA Ops:
  7.2 80.9 %copy-start = (bf16[512,1920]{1,0:T(8,128)(2,1)S(1)}, bf16[512,1920]{1,0:T(8,128)(2,1)}, u32[]{:S(2)}) copy-start(bf16[512,1920]{1,0:T(8,128)(2,1)} %param.12) | copy-start | bytes 5898244
  7.2 2.8 copy-start.1
  7.2 2.9 copy-start.4
  7.2 155.7 %all-reduce.6.cloned.1.call-start = ((), (), s32[]{:S(2)}) async-start(), calls=%async_computation.3 | async-start | bytes 1474560 | tf_op jit(solution)/shard_map/psum | solution.py:27
  9.9 318.3 %all-reduce.10.cloned.1.call-start = ((), (), s32[]{:S(2)}) async-start(), calls=%async_computation.7 | async-start | bytes 3047424 | tf_op jit(solution)/shard_map/psum | solution.py:28
  179.6 226.8 %all-gather.4.cloned.1.call-start = ((), (), s32[]{:S(2)}) async-start(), calls=%async_computation.1 | async-start | bytes 3244032 | tf_op jit(solution)/shard_map/all_gather | solution.py:40
  180.4 280.0 %all-gather.6.cloned.1.call-start = ((), (), s32[]{:S(2)}) async-start(), calls=%async_computation.2 | async-start | bytes 9437184 | tf_op jit(solution)/shard_map/all_gather | solution.py:49
  180.9 308.3 %all-gather.8.cloned.1.call-start = ((), (), s32[]{:S(2)}) async-start(), calls=%async_computation.4 | async-start | bytes 1769472 | tf_op jit(solution)/shard_map/all_gather | solution.py:42
  331.3 157.9 %copy-start.3 = (bf16[192,1536]{0,1:T(8,128)(2,1)S(1)}, bf16[192,1536]{0,1:T(8,128)(2,1)}, u32[]{:S(2)}) copy-start(bf16[192,1536]{0,1:T(8,128)(2,1)} %get-tuple-element.5) | copy-start | bytes 1769476
  331.3 313.8 %all-reduce.8.cloned.1.call-start = ((), (), s32[]{:S(2)}) async-start(), calls=%async_computation.6 | async-start | bytes 1572864 | tf_op jit(solution)/shard_map/psum | solution.py:54
  489.2 2.9 copy-start.2
  489.2 2.9 copy-start.5
  492.1 2.7 copy-start.6
  494.8 370.2 %reduce-scatter.2.cloned.1.call-start = ((), (), s32[]{:S(2)}) async-start(), calls=%async_computation.5 | async-start | bytes 3244032 | tf_op jit(solution)/shard_map/reduce_scatter | solution.py:64
Sparse Core Ops, SparseCore 0:
  11.4 151.4 all-reduce.5
  179.7 148.4 all-reduce.9
  331.0 75.3 all-gather.3
  408.3 51.9 all-gather.5
  462.7 26.4 all-gather.7
  494.9 150.1 all-reduce.7
  649.5 215.4 reduce-scatter.1
where the time goes:
time: 874 us
  waiting for transfers between devices  735 us (84%)
  blocking collectives  91.3 us (10%)
  matrix products  33.1 us (4%)
  between operations  14.2 us (2%)
    reduce_scatter x1, waiting for transfers between devices, shards(): lax.psum_scatter(partial_value.astype(jnp.bfloat16), 'mp', scatter_dimens...  220 us
    psum x1, waiting for transfers between devices, shards(): lax.psum(grad_proj.astype(jnp.bfloat16), 'mp').astype(jnp.float32)  147 us
    psum x1, waiting for transfers between devices, shards(): lax.psum(jnp.dot(cotangent, grads_all.T, preferred_element_type=jnp.float...  142 us
    psum x1, blocking collectives, shards(): input_total, grad_total = lax.psum((input_sq, grad_sq), 'mp')  77.8 us
    all_gather x1, waiting for transfers between devices, shards(): whole_in = lax.all_gather(inputs, 'mp', axis=1, tiled=True)  75 us
    psum x1, waiting for transfers between devices, shards(): lax.psum(input_proj.astype(jnp.bfloat16), 'mp').astype(jnp.float32)  73.4 us
    all_gather x1, waiting for transfers between devices, shards(): lax.all_gather(weight, 'dp', axis=0, tiled=True)  53.9 us
    all_gather x1, waiting for transfers between devices, shards(): grads_all = lax.all_gather(edited_grad, 'dp', axis=0, tiled=True)  22 us
  transfers between devices with their start and end apart: 7, of which 7 were waited for; matrix products, arithmetic and copies ran while one was open for 2% of the time, Pallas kernels for 0%

commit v1 on v0

--- a/solution.py
+++ b/solution.py
@@ -7,6 +7,13 @@
 FW = 16384
 epsilon = 1e-06
 step_size = 0.25
+
+
+def gather_over(block, mesh_axis, dim):
+    n_dev = lax.axis_size(mesh_axis)
+    parts = jnp.stack([block for _ in range(n_dev)])
+    parts = lax.all_to_all(parts, mesh_axis, split_axis=0, concat_axis=0)
+    return jnp.concatenate(parts, axis=dim)
 
 
 def silu_slope(value):
@@ -37,7 +44,7 @@
     edited_grad = (
         grad_wide + jnp.dot(grad_hidden, dec_out, preferred_element_type=jnp.float32)
     ).astype(jnp.bfloat16)
-    whole_in = lax.all_gather(inputs, "mp", axis=1, tiled=True)
+    whole_in = gather_over(inputs, "mp", 1)
     edits_all = lax.all_gather(edited_in, "dp", axis=0, tiled=True)
     grads_all = lax.all_gather(edited_grad, "dp", axis=0, tiled=True)
     kernel = lax.psum(

time: 874 us -> 767 us (0.88)
  waiting for transfers between devices: 735 us -> 616 us
    all_gather x1 -> x0, waiting for transfers between devices: 75 us -> none  [shards(): whole_in = lax.all_gather(inputs, 'mp', axis=1, tiled=True)]
    all_gather x1, waiting for transfers between devices: 53.9 us -> 0.01 us  [shards(): lax.all_gather(weight, 'dp', axis=0, tiled=True)]
    psum x1, waiting for transfers between devices: 147 us -> 170 us  [shards(): lax.psum(grad_proj.astype(jnp.bfloat16), 'mp').astype(jnp.float32)]
    all_gather x1, waiting for transfers between devices: 22 us -> 11.3 us  [shards(): grads_all = lax.all_gather(edited_grad, 'dp', axis=0, tiled=True)]
  transfers between devices with their start and end apart: 7 -> 7, of which waited for: 7 -> 5; matrix products, arithmetic and copies ran while one was open for 2% -> 3% of each run, Pallas kernels for 0% -> 0%
where the time goes in v1:
time: 767 us; the launch traced here: 766 us
  waiting for transfers between devices  616 us (80%)
  blocking collectives  91.3 us (12%)
  matrix products  31.6 us (4%)
  between operations  15.3 us (2%)
    reduce_scatter x1, waiting for transfers between devices, shards(): lax.psum_scatter(partial_value.astype(jnp.bfloat16), 'mp', scatter_dimens...  220 us
    psum x1, waiting for transfers between devices, shards(): lax.psum(grad_proj.astype(jnp.bfloat16), 'mp').astype(jnp.float32)  170 us
    psum x1, waiting for transfers between devices, shards(): lax.psum(jnp.dot(cotangent, grads_all.T, preferred_element_type=jnp.float...  141 us
    psum x1, blocking collectives, shards(): input_total, grad_total = lax.psum((input_sq, grad_sq), 'mp')  77.8 us
    psum x1, waiting for transfers between devices, shards(): lax.psum(input_proj.astype(jnp.bfloat16), 'mp').astype(jnp.float32)  73.4 us
  transfers between devices with their start and end apart: 7, of which 5 were waited for; matrix products, arithmetic and copies ran while one was open for 3% of the time, Pallas kernels for 0%

profile of v1, /device:TPU:8, one launch (start us, length us, event | category | flops | bytes accessed | tf_op | source)
XLA Modules:
  0.0 766.2 jit_solution(4736075670951551556)
XLA Ops:
  8.1 2.7 convolution_convert_fusion.3
  10.8 0.1 fusion.12
  10.9 0.1 fusion.10
  11.1 77.8 %all-reduce = (f32[192]{0:T(256)S(1)}, f32[192]{0:T(256)S(1)}) all-reduce(f32[192]{0:T(256)S(1)} %fusion.10, f32[192]{0:T(256)S(1)} %fusion.12), channel_id=1, replica_groups=mesh['mp'=32,'dp'=8] {'mp'}, use_global_device_ids=true, to_apply=%region_6.7 | all-reduce | flops 384 | bytes 3072 | tf_op jit(solution)/shard_map/psum | solution.py:32
  88.9 1.5 convolution_convert_fusion.1
  90.3 73.4 %all-reduce.6.cloned.1.call-done = bf16[192,1920]{1,0:T(8,128)(2,1)} async-done(((bf16[192,1920]{1,0:T(8,128)(2,1)}), bf16[192,1920]{1,0:T(8,128)(2,1)}) %all-reduce.6.cloned.1.call-update) | async-done | bytes 737296 | tf_op jit(solution)/shard_map/psum | solution.py:34
  163.8 1.8 fusion.2
  165.6 13.5 %all_gather.11 = bf16[1536,256]{1,0:T(8,128)(2,1)S(1)} all-gather(bf16[192,256]{1,0:T(8,128)(2,1)S(1)} %fusion.2), channel_id=1, replica_groups=mesh['mp'=32,'dp'=8] {'dp'}, dimensions={0}, use_global_device_ids=true | all-gather | bytes 884736 | tf_op jit(solution)/shard_map/all_gather | solution.py:48
  179.2 1.2 fusion
  180.5 0.5 all-gather.3.cloned.1.call-update
  181.0 2.1 stack.2
  183.1 5.5 all-to-all-start
  188.5 0.0 all-gather.5.cloned.1.call-start
  188.6 169.7 %all-reduce.10.cloned.1.call-done = (bf16[192,1920]{1,0:T(8,128)(2,1)}, bf16[192,1536]{1,0:T(8,128)(2,1)}) async-done(((bf16[192,1920]{1,0:T(8,128)(2,1)}, bf16[192,1536]{1,0:T(8,128)(2,1)}), (bf16[192,1920]{1,0:T(8,128)(2,1)}, bf16[192,1536]{1,0:T(8,128)(2,1)})) %all-reduce.10.cloned.1.call-update) | async-done | bytes 1327120 | tf_op jit(solution)/shard_map/psum | solution.py:35
  358.3 3.1 fusion.1
  361.5 4.0 copy.10
  365.4 6.9 fusion.20
  372.4 11.3 %all-gather.5.cloned.1.call-done = bf16[1536,512]{1,0:T(8,128)(2,1)} async-done(((bf16[192,512]{1,0:T(8,128)(2,1)}), bf16[1536,512]{1,0:T(8,128)(2,1)}) %all-gather.5.cloned.1.call-update) | async-done | bytes 1572880 | tf_op jit(solution)/shard_map/all_gather | solution.py:49
  383.7 2.9 fusion.19
  386.6 1.5 convolution_convert_fusion.4
  388.2 8.0 %convolution_convert_fusion = bf16[192,8192]{1,0:T(8,128)(2,1)} fusion(bf16[8192,512]{1,0:T(8,128)(2,1)} %all-gather.3.cloned.1.call-done, bf16[192,512]{1,0:T(8,128)(2,1)S(1)} %copy-done.3, f32[192,512]{1,0:T(8,128)S(1)} %get-tuple-element.7), kind=kOutput, calls=%fused_computation | convolution fusion | flops 1613168640 | bytes 12124160 | tf_op jit(solution)/shard_map/dot_general | solution.py:66
  396.2 141.3 %all-reduce.8.cloned.1.call-done = bf16[192,1536]{1,0:T(8,128)(2,1)} async-done(((bf16[192,1536]{1,0:T(8,128)(2,1)}), bf16[192,1536]{1,0:T(8,128)(2,1)}) %all-reduce.8.cloned.1.call-update) | async-done | bytes 589840 | tf_op jit(solution)/shard_map/psum | solution.py:61
  537.5 219.6 %reduce-scatter.2.cloned.1.call-done = bf16[192,256]{1,0:T(8,128)(2,1)} async-done(((bf16[192,8192]{1,0:T(8,128)(2,1)}), bf16[192,256]{1,0:T(8,128)(2,1)}) %reduce-scatter.2.cloned.1.call-update) | async-done | bytes 98320 | tf_op jit(solution)/shard_map/reduce_scatter | solution.py:71
  757.1 2.0 fusion.3
  (22 shorter events, 0.3 us)
Async XLA Ops:
  8.0 80.9 %copy-start = (bf16[512,1920]{1,0:T(8,128)(2,1)S(1)}, bf16[512,1920]{1,0:T(8,128)(2,1)}, u32[]{:S(2)}) copy-start(bf16[512,1920]{1,0:T(8,128)(2,1)} %param.12) | copy-start | bytes 5898244
  8.0 2.8 copy-start.1
  8.0 2.9 copy-start.3
  8.0 155.7 %all-reduce.6.cloned.1.call-start = ((), (), s32[]{:S(2)}) async-start(), calls=%async_computation.3 | async-start | bytes 1474560 | tf_op jit(solution)/shard_map/psum | solution.py:34
  10.8 347.5 %all-reduce.10.cloned.1.call-start = ((), (), s32[]{:S(2)}) async-start(), calls=%async_computation.7 | async-start | bytes 2654208 | tf_op jit(solution)/shard_map/psum | solution.py:35
  180.4 185.0 %all-gather.3.cloned.1.call-start = ((), (), s32[]{:S(2)}) async-start(), calls=%async_computation.2 | async-start | bytes 9437184 | tf_op jit(solution)/shard_map/all_gather | solution.py:56
  183.1 178.4 %all-to-all-start = ((bf16[32,192,256]{2,1,0:T(8,128)(2,1)}), bf16[32,192,256]{2,1,0:T(8,128)(2,1)}, u32[]{:S(2)}, u32[]{:S(2)}) async-start(bf16[32,192,256]{2,1,0:T(8,128)(2,1)} %stack.2), calls=%async_computation | async-start | bytes 6291456 | tf_op jit(solution)/shard_map/all_to_all | solution.py:15
  188.5 195.1 %all-gather.5.cloned.1.call-start = ((), (), s32[]{:S(2)}) async-start(), calls=%async_computation.4 | async-start | bytes 1769472 | tf_op jit(solution)/shard_map/all_gather | solution.py:49
  361.4 176.1 %all-reduce.8.cloned.1.call-start = ((), (), s32[]{:S(2)}) async-start(), calls=%async_computation.6 | async-start | bytes 1179648 | tf_op jit(solution)/shard_map/psum | solution.py:61
  383.7 2.9 copy-start.2
  388.1 368.9 %reduce-scatter.2.cloned.1.call-start = ((), (), s32[]{:S(2)}) async-start(), calls=%async_computation.5 | async-start | bytes 3244032 | tf_op jit(solution)/shard_map/reduce_scatter | solution.py:71
Sparse Core Ops, SparseCore 0:
  12.3 151.4 all-reduce.5
  180.5 177.7 all-reduce.9
  388.3 149.1 all-reduce.7
  541.2 215.8 reduce-scatter.1
Sparse Core Ops, SparseCore 1:
  182.7 47.8 all-gather.2
  361.5 22.1 all-gather.4
